TPU v7x, 32 devices: a whole 2x2x4 slice. The times are simulated.
32 devices in a mesh: dp: 4 (over y, x), section: 2 (over core), tensor: 4 (over z).
Axes of the slice: x: 2, y: 2, z: 4, core: 2. Of those that a mesh axis runs over, the one named last changes fastest.
Arguments:
- tokens: bfloat16 [512, 16384], P('dp'), may hold values from -9 to 9
- order: int32 [512], replicated, may hold values from 0 to 511, as said below
- segments: int32 [512], replicated, may hold values from 0 to 1, as said below
- gain: float32 [2, 16384], P('section', 'dp'), may hold values from 0.1 to 1.9
- w_query: bfloat16 [2, 16384, 8192], P('section', 'dp', 'tensor'), may hold values from -0.046875 to 0.046875
- key_value_weight: bfloat16 [2, 16384, 8, 256], P('section', 'dp', 'tensor'), may hold values from -0.046875 to 0.046875
- w_out: bfloat16 [2, 8192, 16384], P('section', 'tensor', 'dp'), may hold values from -0.0625 to 0.0625
Outputs:
- layer_out: bfloat16 [512, 16384], P('section', 'dp')
Inputs may be any that keep to these rules, and one draw needn't show every extreme that they name: A permutation that moves whole sentences: the rows of one sentence (a run of equal segments within a block of 32 rows) come from consecutive entry rows in order. `segments`: within each block of 32 rows the sentence numbers do not fall and each of 0 to 1 appears.
All inputs are finite; a program needn't handle non-finite values.
Results may differ from a plain program's by a relative error of at most 0.022.
Values may be sent and summed in bfloat16 or wider, within the bound.
A program may use at most 128 MiB of HBM per device.

v0:
```python
import math

import jax
import jax.numpy as jnp
from jax import lax
from jax.sharding import PartitionSpec as P

MODEL_WIDTH = 16384
KEYVALUE_HEADS = 8
QUERY_HEADS = 64
MICRO_TOKENS = 32
M = 4


norm_epsilon = 1e-05


def passed_along(array, axis, by):
    count = lax.axis_size(axis)
    return lax.ppermute(array, axis, [(i, (i + by) % count) for i in range(count)])


def causal_block_attend(query_rows, key_value_rows, sentence_segment_rows, query_group_width):
    row_count = query_rows.shape[0]
    kv_heads = key_value_rows.shape[1]
    head_size = key_value_rows.shape[2] // 2
    query_head_rows = query_rows.reshape(row_count, kv_heads, query_group_width, head_size)
    key_heads = key_value_rows[:, :, :head_size]
    value_heads = key_value_rows[:, :, head_size:]
    scores = jnp.einsum(
        "qkgd,skd->kgqs", query_head_rows, key_heads, preferred_element_type=jnp.float32
    ) / math.sqrt(head_size)
    position = jnp.arange(row_count)
    allowed = (sentence_segment_rows[:, None] == sentence_segment_rows[None, :]) & (
        position[None, :] <= position[:, None]
    )
    raw_weights = jnp.where(allowed[None, None], jnp.exp(scores), 0.0)
    totals = jnp.sum(raw_weights, axis=-1, keepdims=True)
    probs = (raw_weights / totals).astype(jnp.bfloat16)
    attended_rows = jnp.einsum(
        "kgqs,skd->qkgd", probs, value_heads, preferred_element_type=jnp.float32
    )
    return attended_rows.astype(jnp.bfloat16).reshape(
        row_count, kv_heads * query_group_width * head_size
    )


def section_layer(
    hidden, sentence_segment_rows, gain_row, query_weight, key_value_matrix, out_weight
):
    slice_width = hidden.shape[1]
    own_rows = sentence_segment_rows.shape[0]
    own_start = lax.axis_index("dp") * own_rows
    widened = hidden.astype(jnp.float32)
    normed_rows = (widened * gain_row[None, :]).astype(jnp.bfloat16)
    query_terms = jnp.dot(normed_rows, query_weight, preferred_element_type=jnp.float32)
    keyval_terms = jnp.dot(
        normed_rows, key_value_matrix.reshape(slice_width, -1), preferred_element_type=jnp.float32
    )
    square_terms = jnp.sum(widened * widened, axis=1)
    all_squares = lax.psum(square_terms, "dp")
    own_squares = lax.dynamic_slice_in_dim(all_squares, own_start, own_rows)
    query_sums, keyval_sums = (
        lax.psum_scatter(
            query_terms.astype(jnp.bfloat16), "dp", scatter_dimension=0, tiled=True
        ).astype(jnp.float32),
        lax.psum_scatter(
            keyval_terms.astype(jnp.bfloat16), "dp", scatter_dimension=0, tiled=True
        ).astype(jnp.float32),
    )
    root_mean_square = jnp.sqrt(own_squares / MODEL_WIDTH + norm_epsilon)
    query_rows = (query_sums / root_mean_square[:, None]).astype(jnp.bfloat16)
    kv_heads = key_value_matrix.shape[1]
    key_value_rows = (
        (keyval_sums / root_mean_square[:, None])
        .astype(jnp.bfloat16)
        .reshape(own_rows, kv_heads, key_value_matrix.shape[2])
    )
    attended_rows = causal_block_attend(
        query_rows, key_value_rows, sentence_segment_rows, QUERY_HEADS // KEYVALUE_HEADS
    )
    head_terms = jnp.dot(
        lax.all_gather(attended_rows, "dp", axis=0, tiled=True),
        out_weight,
        preferred_element_type=jnp.float32,
    )
    head_total = lax.psum(head_terms.astype(jnp.bfloat16), "tensor").astype(jnp.float32)
    return (widened + head_total).astype(jnp.bfloat16)


def on_device(tokens, order, segments, gain, w_query, key_value_weight, w_out):
    spread = lax.all_to_all(tokens, "dp", split_axis=1, concat_axis=0, tiled=True)
    arranged = jnp.take(spread, order, axis=0)
    group_count = lax.axis_size("dp")
    rows_all = group_count * MICRO_TOKENS
    section_index = lax.axis_index("section")
    group_index = lax.axis_index("dp")
    gain_row = gain[0]
    query_weight = w_query[0]
    key_value_matrix = key_value_weight[0]
    out_weight = w_out[0]
    received = jnp.zeros((rows_all, arranged.shape[1]), jnp.bfloat16)
    inbox = []
    results = []
    for turn_index in range(M + 1):
        if turn_index < M:
            fresh = arranged[turn_index * rows_all : (turn_index + 1) * rows_all]
        else:
            fresh = jnp.zeros_like(received)
        micro_index = jnp.where(
            section_index == 0, min(turn_index, M - 1), max(turn_index - 1, 0)
        ).astype(jnp.int32)
        sentence_segment_rows = lax.dynamic_slice_in_dim(
            segments, micro_index * rows_all + group_index * MICRO_TOKENS, MICRO_TOKENS
        )
        layer_input = jnp.where(section_index == 0, fresh, received)
        layer_output = section_layer(
            layer_input, sentence_segment_rows, gain_row, query_weight, key_value_matrix, out_weight
        )
        inbox.append(received)
        results.append(layer_output)
        if turn_index < M:
            received = passed_along(layer_output, "section", 1)
    half_count = M // 2
    from_back = jnp.concatenate(
        [inbox[index_value + 2] for index_value in range(half_count)], axis=0
    )
    kept_here = jnp.concatenate(
        [results[index_value + 1] for index_value in range(half_count, M)], axis=0
    )
    return jnp.where(section_index == 0, from_back, kept_here)


def solution(mesh):
    placed = (
        P("dp", None),
        P(),
        P(),
        P("section", "dp"),
        P("section", "dp", "tensor"),
        P("section", "dp", "tensor", None),
        P("section", "tensor", "dp"),
    )
    return jax.shard_map(
        on_device, mesh=mesh, in_specs=placed, out_specs=P("section", "dp"), check_vma=False
    )
```

profile of v0, /device:TPU:1, one launch (start us, length us, event | category | flops | bytes accessed | tf_op | source)
XLA Modules:
  0.0 746.0 jit_solution(1543318865760451995)
XLA Ops:
  6.5 4.7 copy.128
  11.2 4.8 all-to-all-start
  16.1 4.8 copy.81
  21.0 42.8 %all-to-all-done = bf16[128,4,4096]{2,0,1:T(8,128)(2,1)} async-done(((bf16[128,4,4096]{2,0,1:T(8,128)(2,1)}), bf16[128,4,4096]{2,0,1:T(8,128)(2,1)}, u32[]{:S(2)}, u32[]{:S(2)}) %all-to-all-start) | async-done | bytes 4194336 | tf_op jit(solution)/shard_map/all_to_all | solution.py:92
  63.8 11.3 %gather_fusion = bf16[512,4096]{1,0:T(8,128)(2,1)} fusion(bf16[512,4096]{1,0:T(8,128)(2,1)} %bitcast.1, s32[1024]{0:T(1024)S(1)} %pad_clamp_fusion), kind=kCustom, calls=%fused_computation | custom fusion | bytes 8390656 | tf_op jit(solution)/shard_map/jit(_take)/gather | solution.py:93
  75.1 2.8 broadcast_select_fusion
  77.9 2.0 copy-done.4
  79.8 1.4 convolution_convert_fusion.4
  81.3 9.2 %fusion.35 = bf16[128,2048]{1,0:T(8,128)(2,1)} fusion(bf16[1,4096,2048]{2,1,0:T(8,128)(2,1)} %param.11, f32[4096]{0:T(1024)S(1)} %bitcast.202, bf16[512,4096]{1,0:T(8,128)(2,1)} %copy-done.4, pred[]{:T(512)S(6)} %eq.98), kind=kOutput, calls=%fused_computation.43 | convolution fusion | flops 2149842944 | bytes 18366464 | tf_op jit(solution)/shard_map/dot_general | solution.py:56
  90.8 1.6 fusion.51
  92.4 6.9 psum.70
  99.3 6.5 reduce-scatter.11.cloned.1.call-done
  106.7 27.3 %reduce-scatter.13.cloned.1.call-done = bf16[32,2048]{1,0:T(8,128)(2,1)} async-done(((bf16[128,2048]{1,0:T(8,128)(2,1)}), bf16[32,2048]{1,0:T(8,128)(2,1)}) %reduce-scatter.13.cloned.1.call-update) | async-done | bytes 131088 | tf_op jit(solution)/shard_map/reduce_scatter | solution.py:64
  135.7 8.1 %all_gather.15 = bf16[128,2048]{1,0:T(8,128)(2,1)S(1)} all-gather(bf16[32,2048]{1,0:T(8,128)(2,1)S(1)} %bitcast.216), channel_id=1, replica_groups=mesh['dp'=4,'section'=2,'tensor'=4] {'dp'}, dimensions={0}, use_global_device_ids=true | all-gather | bytes 655360 | tf_op jit(solution)/shard_map/all_gather | solution.py:83
  143.9 9.1 %fusion.20 = bf16[128,4096]{1,0:T(8,128)(2,1)} fusion(bf16[128,2048]{1,0:T(8,128)(2,1)S(1)} %all_gather.15, bf16[1,2048,4096]{2,1,0:T(8,128)(2,1)} %param.13), kind=kOutput, calls=%fused_computation.21 | convolution fusion | flops 2148007936 | bytes 18350080 | tf_op jit(solution)/shard_map/dot_general | solution.py:82
  153.1 54.3 %all-reduce.6.cloned.1.call-done = bf16[128,4096]{1,0:T(8,128)(2,1)} async-done(((bf16[128,4096]{1,0:T(8,128)(2,1)}), bf16[128,4096]{1,0:T(8,128)(2,1)}) %all-reduce.6.cloned.1.call-update) | async-done | bytes 1048592 | tf_op jit(solution)/shard_map/psum | solution.py:87
  207.3 2.0 fusion.52
  209.9 2.3 collective-permute-done
  212.2 1.7 fusion.54
  213.8 1.4 convolution_convert_fusion.3
  215.3 8.9 %fusion.38 = bf16[128,2048]{1,0:T(8,128)(2,1)} fusion(bf16[1,4096,2048]{2,1,0:T(8,128)(2,1)} %param.11, bf16[128,4096]{1,0:T(8,128)(2,1)S(1)} %get-tuple-element.10, f32[4096]{0:T(1024)S(1)} %bitcast.204), kind=kOutput, calls=%fused_computation.44 | convolution fusion | flops 2149318656 | bytes 18366464 | tf_op jit(solution)/shard_map/dot_general | solution.py:56
  224.4 7.8 %psum.72 = f32[128]{0:T(128)S(1)} all-reduce(f32[128]{0:T(128)S(1)} %get-tuple-element.9), channel_id=1, replica_groups=mesh['dp'=4,'section'=2,'tensor'=4] {'dp'}, use_global_device_ids=true, to_apply=%region_8.9 | all-reduce | flops 128 | bytes 1024 | tf_op jit(solution)/shard_map/psum | solution.py:61
  232.3 5.6 reduce-scatter.15.cloned.1.call-done
  238.8 27.0 %reduce-scatter.17.cloned.1.call-done = bf16[32,2048]{1,0:T(8,128)(2,1)} async-done(((bf16[128,2048]{1,0:T(8,128)(2,1)}), bf16[32,2048]{1,0:T(8,128)(2,1)}) %reduce-scatter.17.cloned.1.call-update) | async-done | bytes 131088 | tf_op jit(solution)/shard_map/reduce_scatter | solution.py:64
  267.4 7.9 %all_gather.16 = bf16[128,2048]{1,0:T(8,128)(2,1)S(1)} all-gather(bf16[32,2048]{1,0:T(8,128)(2,1)S(1)} %bitcast.217), channel_id=1, replica_groups=mesh['dp'=4,'section'=2,'tensor'=4] {'dp'}, dimensions={0}, use_global_device_ids=true | all-gather | bytes 655360 | tf_op jit(solution)/shard_map/all_gather | solution.py:83
  275.4 9.1 %fusion.23 = bf16[128,4096]{1,0:T(8,128)(2,1)} fusion(bf16[128,2048]{1,0:T(8,128)(2,1)S(1)} %all_gather.16, bf16[1,2048,4096]{2,1,0:T(8,128)(2,1)} %param.13), kind=kOutput, calls=%fused_computation.22 | convolution fusion | flops 2148007936 | bytes 18350080 | tf_op jit(solution)/shard_map/dot_general | solution.py:82
  284.6 54.3 %all-reduce.8.cloned.1.call-done = bf16[128,4096]{1,0:T(8,128)(2,1)} async-done(((bf16[128,4096]{1,0:T(8,128)(2,1)}), bf16[128,4096]{1,0:T(8,128)(2,1)}) %all-reduce.8.cloned.1.call-update) | async-done | bytes 1048592 | tf_op jit(solution)/shard_map/psum | solution.py:87
  338.9 1.6 fusion.55
  341.0 2.3 collective-permute-done.1
  343.3 1.7 fusion.57
  345.0 1.4 convolution_convert_fusion.2
  346.7 8.9 %fusion.41 = bf16[128,2048]{1,0:T(8,128)(2,1)} fusion(bf16[1,4096,2048]{2,1,0:T(8,128)(2,1)} %param.11, bf16[128,4096]{1,0:T(8,128)(2,1)S(1)} %get-tuple-element.8, f32[4096]{0:T(1024)S(1)} %bitcast.206), kind=kOutput, calls=%fused_computation.45 | convolution fusion | flops 2149318656 | bytes 18366464 | tf_op jit(solution)/shard_map/dot_general | solution.py:56
  355.7 7.8 %psum.74 = f32[128]{0:T(128)S(1)} all-reduce(f32[128]{0:T(128)S(1)} %get-tuple-element.7), channel_id=1, replica_groups=mesh['dp'=4,'section'=2,'tensor'=4] {'dp'}, use_global_device_ids=true, to_apply=%region_14.15 | all-reduce | flops 128 | bytes 1024 | tf_op jit(solution)/shard_map/psum | solution.py:61
  363.6 5.5 reduce-scatter.19.cloned.1.call-done
  369.9 27.4 %reduce-scatter.21.cloned.1.call-done = bf16[32,2048]{1,0:T(8,128)(2,1)} async-done(((bf16[128,2048]{1,0:T(8,128)(2,1)}), bf16[32,2048]{1,0:T(8,128)(2,1)}) %reduce-scatter.21.cloned.1.call-update) | async-done | bytes 131088 | tf_op jit(solution)/shard_map/reduce_scatter | solution.py:64
  397.3 1.0 fusion.99
  399.0 7.9 %all_gather.17 = bf16[128,2048]{1,0:T(8,128)(2,1)S(1)} all-gather(bf16[32,2048]{1,0:T(8,128)(2,1)S(1)} %bitcast.218), channel_id=1, replica_groups=mesh['dp'=4,'section'=2,'tensor'=4] {'dp'}, dimensions={0}, use_global_device_ids=true | all-gather | bytes 655360 | tf_op jit(solution)/shard_map/all_gather | solution.py:83
  407.0 9.1 %fusion.26 = bf16[128,4096]{1,0:T(8,128)(2,1)} fusion(bf16[128,2048]{1,0:T(8,128)(2,1)S(1)} %all_gather.17, bf16[1,2048,4096]{2,1,0:T(8,128)(2,1)} %param.13), kind=kOutput, calls=%fused_computation.23 | convolution fusion | flops 2148007936 | bytes 18350080 | tf_op jit(solution)/shard_map/dot_general | solution.py:82
  416.1 54.3 %all-reduce.10.cloned.1.call-done = bf16[128,4096]{1,0:T(8,128)(2,1)} async-done(((bf16[128,4096]{1,0:T(8,128)(2,1)}), bf16[128,4096]{1,0:T(8,128)(2,1)}) %all-reduce.10.cloned.1.call-update) | async-done | bytes 1048592 | tf_op jit(solution)/shard_map/psum | solution.py:87
  470.5 1.6 fusion.58
  472.6 2.3 collective-permute-done.2
  474.9 2.1 fusion.60
  477.0 1.4 convolution_convert_fusion.1
  478.4 8.9 %fusion.44 = bf16[128,2048]{1,0:T(8,128)(2,1)} fusion(bf16[1,4096,2048]{2,1,0:T(8,128)(2,1)} %param.11, bf16[128,4096]{1,0:T(8,128)(2,1)S(1)} %get-tuple-element.6, f32[4096]{0:T(1024)S(1)} %bitcast.208), kind=kOutput, calls=%fused_computation.46 | convolution fusion | flops 2149318656 | bytes 18366464 | tf_op jit(solution)/shard_map/dot_general | solution.py:56
  487.5 7.8 %psum.76 = f32[128]{0:T(128)S(1)} all-reduce(f32[128]{0:T(128)S(1)} %get-tuple-element.5), channel_id=1, replica_groups=mesh['dp'=4,'section'=2,'tensor'=4] {'dp'}, use_global_device_ids=true, to_apply=%region_20.21 | all-reduce | flops 128 | bytes 1024 | tf_op jit(solution)/shard_map/psum | solution.py:61
  495.4 5.6 reduce-scatter.23.cloned.1.call-done
  501.9 27.1 %reduce-scatter.25.cloned.1.call-done = bf16[32,2048]{1,0:T(8,128)(2,1)} async-done(((bf16[128,2048]{1,0:T(8,128)(2,1)}), bf16[32,2048]{1,0:T(8,128)(2,1)}) %reduce-scatter.25.cloned.1.call-update) | async-done | bytes 131088 | tf_op jit(solution)/shard_map/reduce_scatter | solution.py:64
  529.0 1.0 fusion.100
  530.7 8.2 %all_gather.18 = bf16[128,2048]{1,0:T(8,128)(2,1)S(1)} all-gather(bf16[32,2048]{1,0:T(8,128)(2,1)S(1)} %bitcast.219), channel_id=1, replica_groups=mesh['dp'=4,'section'=2,'tensor'=4] {'dp'}, dimensions={0}, use_global_device_ids=true | all-gather | bytes 655360 | tf_op jit(solution)/shard_map/all_gather | solution.py:83
  538.9 9.1 %fusion.29 = bf16[128,4096]{1,0:T(8,128)(2,1)} fusion(bf16[128,2048]{1,0:T(8,128)(2,1)S(1)} %all_gather.18, bf16[1,2048,4096]{2,1,0:T(8,128)(2,1)} %param.13), kind=kOutput, calls=%fused_computation.24 | convolution fusion | flops 2148007936 | bytes 18350080 | tf_op jit(solution)/shard_map/dot_general | solution.py:82
  548.1 54.3 %all-reduce.12.cloned.1.call-done = bf16[128,4096]{1,0:T(8,128)(2,1)} async-done(((bf16[128,4096]{1,0:T(8,128)(2,1)}), bf16[128,4096]{1,0:T(8,128)(2,1)}) %all-reduce.12.cloned.1.call-update) | async-done | bytes 1048592 | tf_op jit(solution)/shard_map/psum | solution.py:87
  602.4 1.5 fusion.61
  604.4 2.3 collective-permute-done.3
  606.7 3.6 convolution_convert_fusion
  610.3 8.9 %fusion.47 = bf16[128,2048]{1,0:T(8,128)(2,1)} fusion(bf16[1,4096,2048]{2,1,0:T(8,128)(2,1)} %param.11, f32[4096]{0:T(1024)S(1)} %bitcast.210, bf16[128,4096]{1,0:T(8,128)(2,1)S(1)} %collective-permute-done.3, pred[]{:T(512)S(6)} %eq.98), kind=kOutput, calls=%fused_computation.47 | convolution fusion | flops 2149842944 | bytes 18366464 | tf_op jit(solution)/shard_map/dot_general | solution.py:56
  619.7 7.8 %psum.78 = f32[128]{0:T(128)S(1)} all-reduce(f32[128]{0:T(128)S(1)} %fusion.63), channel_id=1, replica_groups=mesh['dp'=4,'section'=2,'tensor'=4] {'dp'}, use_global_device_ids=true, to_apply=%region_26.27 | all-reduce | flops 128 | bytes 1024 | tf_op jit(solution)/shard_map/psum | solution.py:61
  627.6 5.3 reduce-scatter.27.cloned.1.call-done
  633.8 27.2 %reduce-scatter.29.cloned.1.call-done = bf16[32,2048]{1,0:T(8,128)(2,1)} async-done(((bf16[128,2048]{1,0:T(8,128)(2,1)}), bf16[32,2048]{1,0:T(8,128)(2,1)}) %reduce-scatter.29.cloned.1.call-update) | async-done | bytes 131088 | tf_op jit(solution)/shard_map/reduce_scatter | solution.py:64
  661.0 1.0 fusion.101
  662.7 8.0 %all_gather.19 = bf16[128,2048]{1,0:T(8,128)(2,1)S(1)} all-gather(bf16[32,2048]{1,0:T(8,128)(2,1)S(1)} %bitcast.220), channel_id=1, replica_groups=mesh['dp'=4,'section'=2,'tensor'=4] {'dp'}, dimensions={0}, use_global_device_ids=true | all-gather | bytes 655360 | tf_op jit(solution)/shard_map/all_gather | solution.py:83
  670.7 9.1 %fusion.32 = bf16[128,4096]{1,0:T(8,128)(2,1)} fusion(bf16[128,2048]{1,0:T(8,128)(2,1)S(1)} %all_gather.19, bf16[1,2048,4096]{2,1,0:T(8,128)(2,1)} %param.13), kind=kOutput, calls=%fused_computation.25 | convolution fusion | flops 2148007936 | bytes 18350080 | tf_op jit(solution)/shard_map/dot_general | solution.py:82
  679.8 54.4 %all-reduce.14.cloned.1.call-done = bf16[128,4096]{1,0:T(8,128)(2,1)} async-done(((bf16[128,4096]{1,0:T(8,128)(2,1)}), bf16[128,4096]{1,0:T(8,128)(2,1)}) %all-reduce.14.cloned.1.call-update) | async-done | bytes 1048592 | tf_op jit(solution)/shard_map/psum | solution.py:87
  734.2 1.5 fusion.64
  735.7 3.3 maximum_select_fusion
  (106 shorter events, 14.1 us)
Async XLA Ops:
  11.2 52.6 %all-to-all-start = ((bf16[128,4,4096]{2,0,1:T(8,128)(2,1)}), bf16[128,4,4096]{2,0,1:T(8,128)(2,1)}, u32[]{:S(2)}, u32[]{:S(2)}) async-start(bf16[128,4,4096]{2,0,1:T(8,128)(2,1)} %bitcast.198), calls=%async_computation | async-start | bytes 8388608 | tf_op jit(solution)/shard_map/all_to_all | solution.py:92
  16.0 89.8 %reduce-scatter.11.cloned.1.call-start = ((), (), s32[]{:S(2)}) async-start(), calls=%async_computation.11 | async-start | bytes 163840 | tf_op jit(solution)/shard_map/reduce_scatter | solution.py:67
  16.1 4.9 copy-start.7
  75.1 4.8 copy-start
  75.1 4.8 copy-start.6
  77.9 2.0 copy-start.4
  81.2 9.4 %copy-start.8 = (s32[512]{0:T(512)S(1)}, s32[512]{0:T(512)}, u32[]{:S(2)}) copy-start(s32[512]{0:T(512)} %param.9) | copy-start | bytes 6148
  81.2 52.8 %reduce-scatter.13.cloned.1.call-start = ((), (), s32[]{:S(2)}) async-start(), calls=%async_computation.12 | async-start | bytes 655360 | tf_op jit(solution)/shard_map/reduce_scatter | solution.py:64
  90.6 116.8 %all-reduce.6.cloned.1.call-start = ((), (), s32[]{:S(2)}) async-start(), calls=%async_computation.13 | async-start | bytes 2097152 | tf_op jit(solution)/shard_map/psum | solution.py:87
  153.0 84.9 %reduce-scatter.15.cloned.1.call-start = ((), (), s32[]{:S(2)}) async-start(), calls=%async_computation.14 | async-start | bytes 163840 | tf_op jit(solution)/shard_map/reduce_scatter | solution.py:67
  207.3 6.5 copy-start.1
  209.3 2.8 collective-permute-start
  215.3 50.4 %reduce-scatter.17.cloned.1.call-start = ((), (), s32[]{:S(2)}) async-start(), calls=%async_computation.15 | async-start | bytes 655360 | tf_op jit(solution)/shard_map/reduce_scatter | solution.py:64
  224.2 114.6 %all-reduce.8.cloned.1.call-start = ((), (), s32[]{:S(2)}) async-start(), calls=%async_computation.16 | async-start | bytes 2097152 | tf_op jit(solution)/shard_map/psum | solution.py:87
  284.5 84.5 %reduce-scatter.19.cloned.1.call-start = ((), (), s32[]{:S(2)}) async-start(), calls=%async_computation.17 | async-start | bytes 163840 | tf_op jit(solution)/shard_map/reduce_scatter | solution.py:67
  338.9 6.1 copy-start.2
  340.5 2.8 collective-permute-start.1
  346.4 50.9 %reduce-scatter.21.cloned.1.call-start = ((), (), s32[]{:S(2)}) async-start(), calls=%async_computation.18 | async-start | bytes 655360 | tf_op jit(solution)/shard_map/reduce_scatter | solution.py:64
  355.6 114.8 %all-reduce.10.cloned.1.call-start = ((), (), s32[]{:S(2)}) async-start(), calls=%async_computation.19 | async-start | bytes 2097152 | tf_op jit(solution)/shard_map/psum | solution.py:87
  416.1 84.9 %reduce-scatter.23.cloned.1.call-start = ((), (), s32[]{:S(2)}) async-start(), calls=%async_computation.20 | async-start | bytes 163840 | tf_op jit(solution)/shard_map/reduce_scatter | solution.py:67
  470.5 6.5 copy-start.3
  472.1 2.8 collective-permute-start.2
  474.9 3.5 copy-start.5
  478.4 50.6 %reduce-scatter.25.cloned.1.call-start = ((), (), s32[]{:S(2)}) async-start(), calls=%async_computation.21 | async-start | bytes 655360 | tf_op jit(solution)/shard_map/reduce_scatter | solution.py:64
  487.4 115.0 %all-reduce.12.cloned.1.call-start = ((), (), s32[]{:S(2)}) async-start(), calls=%async_computation.22 | async-start | bytes 2097152 | tf_op jit(solution)/shard_map/psum | solution.py:87
  548.0 84.9 %reduce-scatter.27.cloned.1.call-start = ((), (), s32[]{:S(2)}) async-start(), calls=%async_computation.23 | async-start | bytes 163840 | tf_op jit(solution)/shard_map/reduce_scatter | solution.py:67
  603.9 2.8 collective-permute-start.3
  610.3 50.7 %reduce-scatter.29.cloned.1.call-start = ((), (), s32[]{:S(2)}) async-start(), calls=%async_computation.24 | async-start | bytes 655360 | tf_op jit(solution)/shard_map/reduce_scatter | solution.py:64
  619.3 114.9 %all-reduce.14.cloned.1.call-start = ((), (), s32[]{:S(2)}) async-start(), calls=%async_computation.25 | async-start | bytes 2097152 | tf_op jit(solution)/shard_map/psum | solution.py:87
Sparse Core Ops, SparseCore 0:
  81.4 24.3 reduce-scatter.10
  108.9 25.1 reduce-scatter.12
  153.1 54.1 all-reduce.5
  215.4 22.4 reduce-scatter.14
  240.5 25.1 reduce-scatter.16
  284.6 54.2 all-reduce.7
  346.6 22.4 reduce-scatter.18
  372.1 25.1 reduce-scatter.20
  416.2 54.2 all-reduce.9
  478.5 22.4 reduce-scatter.22
  503.8 25.1 reduce-scatter.24
  548.1 54.2 all-reduce.11
  610.4 22.4 reduce-scatter.26
  635.8 25.1 reduce-scatter.28
  679.9 54.2 all-reduce.13
where the time goes:
time: 755 us; the launch traced here: 746 us
  waiting for transfers between devices  488 us (65%)
  matrix products  102 us (14%)
  blocking collectives  78.3 us (10%)
  other arithmetic  31.5 us (4%)
  local copies, waits for them, and re-layouts  23.6 us (3%)
  between operations  14.2 us (2%)
  starting transfers between devices  7.79 us (1%)
    psum x5, waiting for transfers between devices, section_layer(): lax.psum(head_terms.astype(jnp.bfloat16), 'tensor').astype(jnp.float32)  272 us
    reduce_scatter x5, waiting for transfers between devices, section_layer(): lax.psum_scatter(query_terms.astype(jnp.bfloat16), 'dp', scatter_dimensio...  136 us
    dot_general x5, matrix products, section_layer(): jnp.dot(lax.all_gather(attended_rows, 'dp', axis=0, tiled=True), out_weig...  45.5 us
    dot_general x5, matrix products, section_layer(): jnp.dot(normed_rows, query_weight, preferred_element_type=jnp.float32)  44.9 us
    all_to_all x1, waiting for transfers between devices, on_device(): lax.all_to_all(tokens, 'dp', split_axis=1, concat_axis=0, tiled=True)  42.8 us
    all_gather x5, blocking collectives, section_layer(): lax.all_gather(attended_rows, 'dp', axis=0, tiled=True)  40.1 us
    psum x5, blocking collectives, section_layer(): all_squares = lax.psum(square_terms, 'dp')  38.2 us
    reduce_scatter x5, waiting for transfers between devices, section_layer(): lax.psum_scatter(keyval_terms.astype(jnp.bfloat16), 'dp', scatter_dimensi...  28.4 us
  transfers between devices with their start and end apart: 20, of which 20 were waited for; matrix products, arithmetic and copies ran while one was open for 8% of the time, Pallas kernels for 0%

commit v1 on v0

v1 whole, which is shorter than its diff:
```python
import functools
import math

import jax
import jax.numpy as jnp
from jax import lax
from jax.experimental import pallas as pl
from jax.experimental.pallas import tpu as pltpu
from jax.sharding import PartitionSpec as P

KEYVALUE_HEADS = 8
QUERY_HEADS = 64
HEAD = 128
BLOCK = 32
M = 4
QCHUNKS = 5
CHUNKS = 8
LAG = 2

norm_epsilon = 1e-05
MESH = pl.DeviceIdType.MESH


def kernel(
    D, T,
    tokens, order_col, seg_col, seg_row, gain, wq, wkv, wo,
    out,
    wqkv_v, wo_v, ent, xb, sc, qp, qr, sqp, sqr, mix, zs, zr,
    w_sem, wo_sem, own_sem, a_s, a_r, q_s, q_r, n_s, n_r, m_s, m_r,
    z_s, z_r, t_s, h_s, h_r, l_s,
):
    d = lax.axis_index("dp")
    s = lax.axis_index("section")
    t = lax.axis_index("tensor")
    R = D * BLOCK
    W = xb.shape[1]
    rows_in = tokens.shape[0]
    wc = W // CHUNKS
    qw = qp.shape[1]
    qc = qw // QCHUNKS
    half = T // 2
    is_left = t < half
    inward = jnp.where(is_left, t + 1, t - 1)
    outward = jnp.where(is_left, t - 1, t + 1)
    outer = jnp.logical_or(t == 0, t == T - 1)
    middle = jnp.logical_or(t == half - 1, t == half)
    kind = jnp.where(middle, 1, 0)
    kv_heads = KEYVALUE_HEADS // T
    group = QUERY_HEADS // KEYVALUE_HEADS
    qcols = kv_heads * group * HEAD
    peers = [lax.rem(d + r, D) for r in range(1, D)]

    def remote(src, dst, ss, rs, **where):
        return pltpu.make_async_remote_copy(
            src_ref=src, dst_ref=dst, send_sem=ss, recv_sem=rs,
            device_id=where, device_id_type=MESH,
        )

    def cols(c, width):
        return pl.ds(pl.multiple_of(c * width, width), width)

    def rows(start, count):
        return pl.ds(pl.multiple_of(start, BLOCK), count)

    def w_copy(j):
        if j < QCHUNKS - 1:
            return pltpu.make_async_copy(
                wq.at[:, pl.ds(j * qc, qc)], wqkv_v.at[:, pl.ds(j * qc, qc)], w_sem.at[j]
            )
        return pltpu.make_async_copy(wkv, wqkv_v.at[:, pl.ds(j * qc, qc)], w_sem.at[j])

    def wo_copy(c):
        return pltpu.make_async_copy(
            wo.at[:, cols(c, wc)], wo_v.at[:, cols(c, wc)], wo_sem.at[c]
        )

    own_tokens = pltpu.make_async_copy(
        tokens.at[:, cols(d, W)], ent.at[rows(d * rows_in, rows_in)], own_sem
    )

    def entry(r):
        peer = peers[r]
        return remote(
            tokens.at[:, cols(peer, W)], ent.at[rows(d * rows_in, rows_in)],
            a_s.at[r], a_r.at[r], dp=peer,
        )

    barrier = pltpu.get_barrier_semaphore()
    for peer in peers:
        pl.semaphore_signal(barrier, inc=1, device_id={"dp": peer}, device_id_type=MESH)
    pl.semaphore_signal(barrier, inc=1, device_id={"section": 1 - s}, device_id_type=MESH)

    @pl.when(t > 0)
    def _():
        pl.semaphore_signal(barrier, inc=1, device_id={"tensor": t - 1}, device_id_type=MESH)

    @pl.when(t < T - 1)
    def _():
        pl.semaphore_signal(barrier, inc=1, device_id={"tensor": t + 1}, device_id_type=MESH)

    pl.semaphore_wait(barrier, D + jnp.where(t > 0, 1, 0) + jnp.where(t < T - 1, 1, 0))

    @pl.when(s == 0)
    def _():
        for r in range(D - 1):
            entry(r).start()
        own_tokens.start()

    for j in range(QCHUNKS):
        w_copy(j).start()
    for c in range(CHUNKS):
        wo_copy(c).start()

    @pl.when(s == 0)
    def _():
        own_tokens.wait()
        for r in range(D - 1):
            entry(r).wait_recv()

    def micro(m, carry):
        slot = lax.rem(m, 2)
        mrow = m * R

        def handed(c):
            return remote(
                xb.at[:, cols(c, wc)], ent.at[rows(mrow, R), cols(c, wc)],
                h_s.at[c], h_r.at[m, c], section=1 - s,
            )

        def finished_away(c):
            return remote(
                xb.at[:, cols(c, wc)], out.at[rows(mrow, R), cols(c, wc)],
                h_s.at[c], h_r.at[m, c], section=1 - s,
            )

        def finished_here(c):
            return pltpu.make_async_copy(
                xb.at[:, cols(c, wc)],
                out.at[rows((m - M // 2) * R, R), cols(c, wc)],
                l_s.at[c],
            )

        @pl.when(s == 0)
        def _():
            width = M * R
            pick = (
                order_col[rows(mrow, R), :]
                == lax.broadcasted_iota(jnp.int32, (R, width), 1)
            ).astype(jnp.float32).astype(jnp.bfloat16)

            def take(c, _):
                xb[:, cols(c, wc)] = jnp.dot(
                    pick, ent[:, cols(c, wc)], preferred_element_type=jnp.float32
                ).astype(jnp.bfloat16)
                return 0

            lax.fori_loop(0, CHUNKS, take, 0)

        @pl.when(s == 1)
        def _():
            def take(c, _):
                handed(c).wait_recv()
                xb[:, cols(c, wc)] = ent[rows(mrow, R), cols(c, wc)]
                return 0

            lax.fori_loop(0, CHUNKS, take, 0)

        def scale(c, total):
            wide = xb[:, cols(c, wc)].astype(jnp.float32)
            sc[:, cols(c, wc)] = (wide * gain[:, cols(c, wc)]).astype(jnp.bfloat16)
            square = wide * wide
            for k in range(wc // 128):
                total = total + square[:, k * 128 : (k + 1) * 128]
            return total

        squares = lax.fori_loop(0, CHUNKS, scale, jnp.zeros((R, 128), jnp.float32))
        sqp[...] = squares

        def norm_copy(r):
            return remote(
                sqp.at[rows(peers[r] * BLOCK, BLOCK)], sqr.at[slot, r],
                n_s.at[r], n_r.at[slot, r], dp=peers[r],
            )

        def q_copy(r, j):
            return remote(
                qp.at[rows(peers[r] * BLOCK, BLOCK), cols(j, qc)],
                qr.at[slot, r, :, cols(j, qc)],
                q_s.at[r, j], q_r.at[slot, r, j], dp=peers[r],
            )

        for r in range(D - 1):
            norm_copy(r).start()

        @pl.when(m == 0)
        def _():
            for j in range(QCHUNKS):
                w_copy(j).wait()

        def project(j, _):
            qp[:, cols(j, qc)] = jnp.dot(
                sc[...], wqkv_v[:, cols(j, qc)], preferred_element_type=jnp.float32
            ).astype(jnp.bfloat16)
            for r in range(D - 1):
                q_copy(r, j).start()
            return 0

        lax.fori_loop(0, QCHUNKS, project, 0)

        own = rows(d * BLOCK, BLOCK)
        for r in range(D - 1):
            norm_copy(r).wait_recv()
        square = sqp[own, :]
        for r in range(D - 1):
            square = square + sqr[slot, r]
        rms = jnp.sqrt(
            jnp.sum(square, axis=1, keepdims=True) / (W * D) + norm_epsilon
        )

        def arrived(j, _):
            for r in range(D - 1):
                q_copy(r, j).wait_recv()
            return 0

        lax.fori_loop(0, QCHUNKS, arrived, 0)

        def summed(start, width):
            total = qp[own, pl.ds(start, width)].astype(jnp.float32)
            for r in range(D - 1):
                total = total + qr[slot, r, :, pl.ds(start, width)].astype(jnp.float32)
            return (total / rms).astype(jnp.bfloat16)

        base = mrow + d * BLOCK
        same = seg_col[rows(base, BLOCK), :] == seg_row[pl.ds(m * D + d, 1), :]
        later = lax.broadcasted_iota(jnp.int32, (BLOCK, BLOCK), 1)
        here = lax.broadcasted_iota(jnp.int32, (BLOCK, BLOCK), 0)
        allowed = jnp.where(jnp.logical_and(same, later <= here), 1, 0)
        allowed = jnp.concatenate([allowed] * group, axis=0) != 0

        def mix_copy(r, h):
            part = mix.at[slot, own, pl.ds(h * group * HEAD, group * HEAD)]
            return remote(
                part, part, m_s.at[r, h], m_r.at[slot, r, h], dp=peers[r]
            )

        for h in range(kv_heads):
            lower = h * group * HEAD
            query = jnp.concatenate(
                [summed(lower + g * HEAD, HEAD) for g in range(group)], axis=0
            )
            key = summed(qcols + h * 2 * HEAD, HEAD)
            value = summed(qcols + h * 2 * HEAD + HEAD, HEAD)
            scores = lax.dot_general(
                query, key, (((1,), (1,)), ((), ())), preferred_element_type=jnp.float32
            ) / math.sqrt(HEAD)
            weights = jnp.where(allowed, jnp.exp(scores), 0.0)
            probs = (weights / jnp.sum(weights, axis=1, keepdims=True)).astype(jnp.bfloat16)
            mixed = jnp.dot(probs, value, preferred_element_type=jnp.float32).astype(
                jnp.bfloat16
            )
            for g in range(group):
                mix[slot, own, pl.ds(lower + g * HEAD, HEAD)] = mixed[
                    g * BLOCK : (g + 1) * BLOCK
                ]
            for r in range(D - 1):
                mix_copy(r, h).start()

        @pl.when(m == 0)
        def _():
            for c in range(CHUNKS):
                wo_copy(c).wait()

        for h in range(kv_heads):
            for r in range(D - 1):
                mix_copy(r, h).wait_recv()

        def inward_copy(c):
            return remote(
                zs.at[:, cols(c, wc)], zr.at[kind, slot, :, cols(c, wc)],
                z_s.at[c], z_r.at[kind, slot, c], tensor=inward,
            )

        def from_outside(c):
            return remote(
                zs.at[:, cols(c, wc)], zr.at[0, slot, :, cols(c, wc)],
                z_s.at[c], z_r.at[0, slot, c], tensor=inward,
            )

        def outward_copy(c):
            return remote(
                xb.at[:, cols(c, wc)], zr.at[1, slot, :, cols(c, wc)],
                t_s.at[c], z_r.at[1, slot, c], tensor=outward,
            )

        def partial(c, _):
            zs[:, cols(c, wc)] = jnp.dot(
                mix[slot], wo_v[:, cols(c, wc)], preferred_element_type=jnp.float32
            ).astype(jnp.bfloat16)

            @pl.when(outer)
            def _():
                inward_copy(c).start()

            return 0

        lax.fori_loop(0, CHUNKS, partial, 0)

        def relay(step, _):
            @pl.when(jnp.logical_and(jnp.logical_not(outer), step < CHUNKS))
            def _():
                from_outside(step).wait_recv()
                zs[:, cols(step, wc)] = (
                    zs[:, cols(step, wc)].astype(jnp.float32)
                    + zr[0, slot, :, cols(step, wc)].astype(jnp.float32)
                ).astype(jnp.bfloat16)
                inward_copy(step).start()

            @pl.when(step >= LAG)
            def _():
                c = step - LAG
                outward_copy(c).wait_recv()

                @pl.when(middle)
                def _():
                    xb[:, cols(c, wc)] = (
                        xb[:, cols(c, wc)].astype(jnp.float32)
                        + (
                            zs[:, cols(c, wc)].astype(jnp.float32)
                            + zr[1, slot, :, cols(c, wc)].astype(jnp.float32)
                        )
                    ).astype(jnp.bfloat16)

                @pl.when(jnp.logical_not(middle))
                def _():
                    xb[:, cols(c, wc)] = zr[1, slot, :, cols(c, wc)]

                @pl.when(jnp.logical_not(outer))
                def _():
                    outward_copy(c).start()

                @pl.when(s == 0)
                def _():
                    handed(c).start()

                @pl.when(jnp.logical_and(s == 1, m < M // 2))
                def _():
                    finished_away(c).start()

                @pl.when(jnp.logical_and(s == 1, m >= M // 2))
                def _():
                    finished_here(c).start()

            return 0

        lax.fori_loop(0, CHUNKS + LAG, relay, 0)

        def sent(c, _):
            inward_copy(c).wait_send()

            @pl.when(jnp.logical_not(outer))
            def _():
                outward_copy(c).wait_send()

            @pl.when(s == 0)
            def _():
                handed(c).wait_send()

            @pl.when(jnp.logical_and(s == 1, m < M // 2))
            def _():
                finished_away(c).wait_send()

            @pl.when(jnp.logical_and(s == 1, m >= M // 2))
            def _():
                finished_here(c).wait()

            return 0

        lax.fori_loop(0, CHUNKS, sent, 0)

        def q_sent(j, _):
            for r in range(D - 1):
                q_copy(r, j).wait_send()
            return 0

        lax.fori_loop(0, QCHUNKS, q_sent, 0)
        for r in range(D - 1):
            norm_copy(r).wait_send()
            for h in range(kv_heads):
                mix_copy(r, h).wait_send()
        return carry

    lax.fori_loop(0, M, micro, 0)

    @pl.when(s == 0)
    def _():
        for r in range(D - 1):
            entry(r).wait_send()

        def returned(i, _):
            m, c = i // CHUNKS, lax.rem(i, CHUNKS)
            remote(
                xb.at[:, cols(c, wc)], out.at[rows(m * R, R), cols(c, wc)],
                h_s.at[c], h_r.at[m, c], section=1 - s,
            ).wait_recv()
            return 0

        lax.fori_loop(0, (M // 2) * CHUNKS, returned, 0)


def on_device(D, T, tokens, order, segments, gain, w_query, key_value_weight, w_out):
    R = D * BLOCK
    W = gain.shape[1]
    qcols = w_query.shape[2]
    wkv = key_value_weight[0].reshape(W, -1)
    qw = qcols + wkv.shape[1]
    kv_heads = key_value_weight.shape[2]
    bf16, f32 = jnp.bfloat16, jnp.float32
    vmem, hbm = pl.BlockSpec(memory_space=pltpu.VMEM), pl.BlockSpec(memory_space=pl.ANY)
    dma = pltpu.SemaphoreType.DMA
    return pl.pallas_call(
        functools.partial(kernel, D, T),
        out_shape=jax.ShapeDtypeStruct((M // 2 * R, W), bf16),
        in_specs=[hbm, vmem, vmem, vmem, vmem, hbm, hbm, hbm],
        out_specs=hbm,
        scratch_shapes=[
            pltpu.VMEM((W, qw), bf16),
            pltpu.VMEM((qcols, W), bf16),
            pltpu.VMEM((M * R, W), bf16),
            pltpu.VMEM((R, W), bf16),
            pltpu.VMEM((R, W), bf16),
            pltpu.VMEM((R, qw), bf16),
            pltpu.VMEM((2, D - 1, BLOCK, qw), bf16),
            pltpu.VMEM((R, 128), f32),
            pltpu.VMEM((2, D - 1, BLOCK, 128), f32),
            pltpu.VMEM((2, R, qcols), bf16),
            pltpu.VMEM((R, W), bf16),
            pltpu.VMEM((2, 2, R, W), bf16),
            dma((QCHUNKS,)),
            dma((CHUNKS,)),
            dma,
            dma((D - 1,)),
            dma((D - 1,)),
            dma((D - 1, QCHUNKS)),
            dma((2, D - 1, QCHUNKS)),
            dma((D - 1,)),
            dma((2, D - 1)),
            dma((D - 1, kv_heads)),
            dma((2, D - 1, kv_heads)),
            dma((CHUNKS,)),
            dma((2, 2, CHUNKS)),
            dma((CHUNKS,)),
            dma((CHUNKS,)),
            dma((M, CHUNKS)),
            dma((CHUNKS,)),
        ],
        compiler_params=pltpu.CompilerParams(
            collective_id=0, has_side_effects=True, vmem_limit_bytes=62 * 1024 * 1024
        ),
    )(
        tokens,
        order[:, None],
        segments[:, None],
        segments.reshape(M * D, BLOCK),
        gain,
        w_query[0],
        wkv,
        w_out[0],
    )


def solution(mesh):
    placed = (
        P("dp", None),
        P(),
        P(),
        P("section", "dp"),
        P("section", "dp", "tensor"),
        P("section", "dp", "tensor", None),
        P("section", "tensor", "dp"),
    )
    return jax.shard_map(
        functools.partial(on_device, mesh.shape["dp"], mesh.shape["tensor"]),
        mesh=mesh, in_specs=placed, out_specs=P("section", "dp"), check_vma=False,
    )
```

time: 755 us -> 272 us (0.36); the launches traced: 746 us -> 271 us
  waiting for transfers between devices: 488 us -> 0 us
  Pallas kernels: 0 us -> 259 us
  matrix products: 102 us -> 0 us
  blocking collectives: 78.3 us -> 0 us
  other arithmetic: 31.5 us -> 0 us
  between operations: 14.2 us -> 0.01 us
  local copies, waits for them, and re-layouts: 23.6 us -> 12.4 us
  starting transfers between devices: 7.79 us -> 0 us
    psum x5 -> x0, waiting for transfers between devices: 272 us -> none  [section_layer(): lax.psum(head_terms.astype(jnp.bfloat16), 'tensor').astype(jnp.float32)]
    pallas_call x0 -> x1, Pallas kernels: none -> 259 us  [on_device(): pl.pallas_call(functools.partial(kernel, D, T), out_shape=jax.ShapeDtypeS...]
    reduce_scatter x10 -> x0, waiting for transfers between devices: 164 us -> none  [the longest x5 136 us: section_layer(): lax.psum_scatter(query_terms.astype(jnp.bfloat16), 'dp', scatter_dimensio...]
    dot_general x25 -> x0, matrix products: 102 us -> none  [the longest x5 45.5 us: section_layer(): jnp.dot(lax.all_gather(attended_rows, 'dp', axis=0, tiled=True), out_weig...]
    all_to_all x1 -> x0, waiting for transfers between devices: 42.8 us -> none  [on_device(): lax.all_to_all(tokens, 'dp', split_axis=1, concat_axis=0, tiled=True)]
    all_gather x5 -> x0, blocking collectives: 40.1 us -> none  [section_layer(): lax.all_gather(attended_rows, 'dp', axis=0, tiled=True)]
    psum x5 -> x0, blocking collectives: 38.2 us -> none  [section_layer(): all_squares = lax.psum(square_terms, 'dp')]
    convert_element_type x10 -> x0, other arithmetic: 12.4 us -> none  [the longest x5 8.24 us: section_layer(): return (widened + head_total).astype(jnp.bfloat16)]
  transfers between devices with their start and end apart: 20 -> 0, of which waited for: 20 -> 0; matrix products, arithmetic and copies ran while one was open for 8% -> 0% of each run, Pallas kernels for 0% -> 0%
where the time goes in v1:
time: 272 us; the launch traced here: 271 us
  Pallas kernels  259 us (95%)
  local copies, waits for them, and re-layouts  12.4 us (5%)
    pallas_call x1, Pallas kernels, on_device(): pl.pallas_call(functools.partial(kernel, D, T), out_shape=jax.ShapeDtypeS...  259 us
    unnamed x2, local copies, waits for them, and re-layouts  7.97 us

profile of v1, /device:TPU:1, one launch (start us, length us, event | category | flops | bytes accessed | tf_op | source)
XLA Modules:
  0.0 271.3 jit_solution(11408027859211001490)
XLA Ops:
  0.0 1.4 reshape.3.seg_row
  1.4 1.5 copy.8.order_col
  2.9 1.5 copy.9.seg_col
  4.4 4.8 %copy.10 = bf16[512,8,2,256]{3,1,2,0:T(8,128)(2,1)} copy(bf16[512,8,2,256]{3,2,1,0:T(2,128)(2,1)} %bitcast.10) | data formatting | bytes 8388608
  9.3 258.8 %shard_map.73 = bf16[256,4096]{1,0:T(8,128)(2,1)} custom-call(bf16[128,16384]{1,0:T(8,128)(2,1)} %tokens.1, s32[512,1]{1,0:T(8,128)} %copy.8.order_col, s32[512,1]{1,0:T(8,128)} %copy.9.seg_col, s32[16,32]{1,0:T(8,128)} %reshape.3.seg_row, f32[1,4096]{1,0:T(1,128)} %gain.1, bf16[4096,2048]{1,0:T(8,128)(2,1)} %bitcast.7, bf16[4096,512]{1,0:T(8,128)(2,1)} %bitcast.9, ...), custom_call_target="tpu_custom_call" | custom-call | tf_op jit(solution)/shard_map/pallas_call | solution.py:420
  268.1 3.1 %copy.12 = bf16[256,4096]{1,0:T(8,128)(2,1)} copy(bf16[256,4096]{1,0:T(8,128)(2,1)} %shard_map.73) | data formatting | bytes 4194304

commit v2 on v1

--- a/solution.py
+++ b/solution.py
@@ -15,6 +15,7 @@
 M = 4
 QCHUNKS = 5
 CHUNKS = 8
+EARLY = 3
 LAG = 2
 
 norm_epsilon = 1e-05
@@ -23,9 +24,9 @@
 
 def kernel(
     D, T,
-    tokens, order_col, seg_col, seg_row, gain, wq, wkv, wo,
+    tokens, order, segments, gain, wq, wkv, wo,
     out,
-    wqkv_v, wo_v, ent, xb, sc, qp, qr, sqp, sqr, mix, zs, zr,
+    wqkv_v, wo_v, ent, pick, xb, sc, qp, qr, sqp, sqr, mix, zs, zr,
     w_sem, wo_sem, own_sem, a_s, a_r, q_s, q_r, n_s, n_r, m_s, m_r,
     z_s, z_r, t_s, h_s, h_r, l_s,
 ):
@@ -33,7 +34,7 @@
     s = lax.axis_index("section")
     t = lax.axis_index("tensor")
     R = D * BLOCK
-    W = xb.shape[1]
+    W = xb.shape[2]
     rows_in = tokens.shape[0]
     wc = W // CHUNKS
     qw = qp.shape[1]
@@ -117,99 +118,124 @@
         for r in range(D - 1):
             entry(r).wait_recv()
 
-    def micro(m, carry):
-        slot = lax.rem(m, 2)
-        mrow = m * R
-
-        def handed(c):
-            return remote(
-                xb.at[:, cols(c, wc)], ent.at[rows(mrow, R), cols(c, wc)],
-                h_s.at[c], h_r.at[m, c], section=1 - s,
-            )
-
-        def finished_away(c):
-            return remote(
-                xb.at[:, cols(c, wc)], out.at[rows(mrow, R), cols(c, wc)],
-                h_s.at[c], h_r.at[m, c], section=1 - s,
-            )
-
-        def finished_here(c):
-            return pltpu.make_async_copy(
-                xb.at[:, cols(c, wc)],
-                out.at[rows((m - M // 2) * R, R), cols(c, wc)],
-                l_s.at[c],
-            )
-
-        @pl.when(s == 0)
-        def _():
-            width = M * R
-            pick = (
-                order_col[rows(mrow, R), :]
-                == lax.broadcasted_iota(jnp.int32, (R, width), 1)
-            ).astype(jnp.float32).astype(jnp.bfloat16)
-
-            def take(c, _):
-                xb[:, cols(c, wc)] = jnp.dot(
-                    pick, ent[:, cols(c, wc)], preferred_element_type=jnp.float32
-                ).astype(jnp.bfloat16)
-                return 0
-
-            lax.fori_loop(0, CHUNKS, take, 0)
-
+    def handed(n, c):
+        return remote(
+            xb.at[lax.rem(n, 2), :, cols(c, wc)], ent.at[rows(n * R, R), cols(c, wc)],
+            h_s.at[c], h_r.at[n, c], section=1 - s,
+        )
+
+    def norm_copy(n, r):
+        return remote(
+            sqp.at[rows(peers[r] * BLOCK, BLOCK)], sqr.at[lax.rem(n, 2), r],
+            n_s.at[r], n_r.at[lax.rem(n, 2), r], dp=peers[r],
+        )
+
+    def q_copy(n, r, j):
+        return remote(
+            qp.at[rows(peers[r] * BLOCK, BLOCK), cols(j, qc)],
+            qr.at[lax.rem(n, 2), r, :, cols(j, qc)],
+            q_s.at[r, j], q_r.at[lax.rem(n, 2), r, j], dp=peers[r],
+        )
+
+    def choose(n):
+        line = order[pl.ds(pl.multiple_of(n * R, R), R)].astype(jnp.float32)[None, :]
+        down = lax.broadcasted_iota(jnp.int32, (R, R), 0)
+        across = lax.broadcasted_iota(jnp.int32, (R, R), 1)
+        column = jnp.sum(jnp.where(down == across, line, 0.0), axis=1, keepdims=True)
+        places = lax.broadcasted_iota(jnp.int32, (R, M * R), 1).astype(jnp.float32)
+        pick[...] = jnp.where(column == places, 1.0, 0.0).astype(jnp.bfloat16)
+
+    def take(n, c):
+        xb[lax.rem(n, 2), :, cols(c, wc)] = jnp.dot(
+            pick[...], ent[:, cols(c, wc)], preferred_element_type=jnp.float32
+        ).astype(jnp.bfloat16)
+
+    def scale(n):
         @pl.when(s == 1)
         def _():
-            def take(c, _):
-                handed(c).wait_recv()
-                xb[:, cols(c, wc)] = ent[rows(mrow, R), cols(c, wc)]
+            def received(c, _):
+                handed(n, c).wait_recv()
+                xb[lax.rem(n, 2), :, cols(c, wc)] = ent[rows(n * R, R), cols(c, wc)]
                 return 0
 
-            lax.fori_loop(0, CHUNKS, take, 0)
-
-        def scale(c, total):
-            wide = xb[:, cols(c, wc)].astype(jnp.float32)
+            lax.fori_loop(0, CHUNKS, received, 0)
+
+        def one(c, total):
+            wide = xb[lax.rem(n, 2), :, cols(c, wc)].astype(jnp.float32)
             sc[:, cols(c, wc)] = (wide * gain[:, cols(c, wc)]).astype(jnp.bfloat16)
             square = wide * wide
             for k in range(wc // 128):
                 total = total + square[:, k * 128 : (k + 1) * 128]
             return total
 
-        squares = lax.fori_loop(0, CHUNKS, scale, jnp.zeros((R, 128), jnp.float32))
-        sqp[...] = squares
-
-        def norm_copy(r):
+        sqp[...] = lax.fori_loop(0, CHUNKS, one, jnp.zeros((R, 128), jnp.float32))
+        for r in range(D - 1):
+            norm_copy(n, r).start()
+
+    def project(n, j):
+        qp[:, cols(j, qc)] = jnp.dot(
+            sc[...], wqkv_v[:, cols(j, qc)], preferred_element_type=jnp.float32
+        ).astype(jnp.bfloat16)
+        for r in range(D - 1):
+            q_copy(n, r, j).start()
+
+    @pl.when(s == 0)
+    def _():
+        choose(0)
+
+        def first_take(c, _):
+            take(0, c)
+            return 0
+
+        lax.fori_loop(0, CHUNKS, first_take, 0)
+
+    scale(0)
+    for j in range(QCHUNKS):
+        w_copy(j).wait()
+
+    def first_project(j, _):
+        project(0, j)
+        return 0
+
+    lax.fori_loop(0, QCHUNKS, first_project, 0)
+
+    own = rows(d * BLOCK, BLOCK)
+
+    def micro(m, carry):
+        slot = lax.rem(m, 2)
+        mrow = m * R
+        xm = xb.at[slot]
+
+        def finished_away(c):
             return remote(
-                sqp.at[rows(peers[r] * BLOCK, BLOCK)], sqr.at[slot, r],
-                n_s.at[r], n_r.at[slot, r], dp=peers[r],
-            )
-
-        def q_copy(r, j):
-            return remote(
-                qp.at[rows(peers[r] * BLOCK, BLOCK), cols(j, qc)],
-                qr.at[slot, r, :, cols(j, qc)],
-                q_s.at[r, j], q_r.at[slot, r, j], dp=peers[r],
-            )
-
-        for r in range(D - 1):
-            norm_copy(r).start()
-
-        @pl.when(m == 0)
-        def _():
-            for j in range(QCHUNKS):
-                w_copy(j).wait()
-
-        def project(j, _):
-            qp[:, cols(j, qc)] = jnp.dot(
-                sc[...], wqkv_v[:, cols(j, qc)], preferred_element_type=jnp.float32
-            ).astype(jnp.bfloat16)
-            for r in range(D - 1):
-                q_copy(r, j).start()
-            return 0
-
-        lax.fori_loop(0, QCHUNKS, project, 0)
-
-        own = rows(d * BLOCK, BLOCK)
-        for r in range(D - 1):
-            norm_copy(r).wait_recv()
+                xm.at[:, cols(c, wc)], out.at[rows(mrow, R), cols(c, wc)],
+                h_s.at[c], h_r.at[m, c], section=1 - s,
+            )
+
+        def finished_here(c):
+            return pltpu.make_async_copy(
+                xm.at[:, cols(c, wc)],
+                out.at[rows((m - M // 2) * R, R), cols(c, wc)],
+                l_s.at[c],
+            )
+
+        line = segments[pl.ds(pl.multiple_of(mrow, R), R)].astype(jnp.float32)[None, :]
+        down = lax.broadcasted_iota(jnp.int32, (BLOCK, R), 0) + d * BLOCK
+        mine = down == lax.broadcasted_iota(jnp.int32, (BLOCK, R), 1)
+        column = jnp.sum(jnp.where(mine, line, 0.0), axis=1, keepdims=True)
+        same = jnp.where(column == line, 1.0, 0.0).astype(jnp.bfloat16)
+        same = lax.dot_general(
+            same, jnp.where(mine, 1.0, 0.0).astype(jnp.bfloat16),
+            (((1,), (1,)), ((), ())), preferred_element_type=jnp.float32,
+        )
+        causal = lax.broadcasted_iota(jnp.int32, (BLOCK, BLOCK), 1) <= (
+            lax.broadcasted_iota(jnp.int32, (BLOCK, BLOCK), 0)
+        )
+        allowed = jnp.where(causal, same, 0.0)
+        allowed = jnp.concatenate([allowed] * group, axis=0) > 0.5
+
+        for r in range(D - 1):
+            norm_copy(m, r).wait_recv()
         square = sqp[own, :]
         for r in range(D - 1):
             square = square + sqr[slot, r]
@@ -219,7 +245,7 @@
 
         def arrived(j, _):
             for r in range(D - 1):
-                q_copy(r, j).wait_recv()
+                q_copy(m, r, j).wait_recv()
             return 0
 
         lax.fori_loop(0, QCHUNKS, arrived, 0)
@@ -229,13 +255,6 @@
             for r in range(D - 1):
                 total = total + qr[slot, r, :, pl.ds(start, width)].astype(jnp.float32)
             return (total / rms).astype(jnp.bfloat16)
-
-        base = mrow + d * BLOCK
-        same = seg_col[rows(base, BLOCK), :] == seg_row[pl.ds(m * D + d, 1), :]
-        later = lax.broadcasted_iota(jnp.int32, (BLOCK, BLOCK), 1)
-        here = lax.broadcasted_iota(jnp.int32, (BLOCK, BLOCK), 0)
-        allowed = jnp.where(jnp.logical_and(same, later <= here), 1, 0)
-        allowed = jnp.concatenate([allowed] * group, axis=0) != 0
 
         def mix_copy(r, h):
             part = mix.at[slot, own, pl.ds(h * group * HEAD, group * HEAD)]
@@ -265,6 +284,19 @@
             for r in range(D - 1):
                 mix_copy(r, h).start()
 
+        def q_sent(j, _):
+            for r in range(D - 1):
+                q_copy(m, r, j).wait_send()
+            return 0
+
+        lax.fori_loop(0, QCHUNKS, q_sent, 0)
+        for r in range(D - 1):
+            norm_copy(m, r).wait_send()
+
+        @pl.when(jnp.logical_and(s == 0, m + 1 < M))
+        def _():
+            choose(m + 1)
+
         @pl.when(m == 0)
         def _():
             for c in range(CHUNKS):
@@ -288,42 +320,62 @@
 
         def outward_copy(c):
             return remote(
-                xb.at[:, cols(c, wc)], zr.at[1, slot, :, cols(c, wc)],
+                xm.at[:, cols(c, wc)], zr.at[1, slot, :, cols(c, wc)],
                 t_s.at[c], z_r.at[1, slot, c], tensor=outward,
             )
 
-        def partial(c, _):
-            zs[:, cols(c, wc)] = jnp.dot(
-                mix[slot], wo_v[:, cols(c, wc)], preferred_element_type=jnp.float32
-            ).astype(jnp.bfloat16)
-
-            @pl.when(outer)
-            def _():
+        def relay(step, _):
+            @pl.when(step < CHUNKS)
+            def _():
+                zs[:, cols(step, wc)] = jnp.dot(
+                    mix[slot], wo_v[:, cols(step, wc)], preferred_element_type=jnp.float32
+                ).astype(jnp.bfloat16)
+
+                @pl.when(outer)
+                def _():
+                    inward_copy(step).start()
+
+                @pl.when(jnp.logical_and(s == 0, m + 1 < M))
+                def _():
+                    take(m + 1, step)
+
+            @pl.when(
+                jnp.logical_and(
+                    jnp.logical_not(outer),
+                    jnp.logical_and(step >= EARLY, step < CHUNKS + EARLY),
+                )
+            )
+            def _():
+                c = step - EARLY
+                from_outside(c).wait_recv()
+                zs[:, cols(c, wc)] = (
+                    zs[:, cols(c, wc)].astype(jnp.float32)
+                    + zr[0, slot, :, cols(c, wc)].astype(jnp.float32)
+                ).astype(jnp.bfloat16)
                 inward_copy(c).start()
 
-            return 0
-
-        lax.fori_loop(0, CHUNKS, partial, 0)
-
-        def relay(step, _):
-            @pl.when(jnp.logical_and(jnp.logical_not(outer), step < CHUNKS))
-            def _():
-                from_outside(step).wait_recv()
-                zs[:, cols(step, wc)] = (
-                    zs[:, cols(step, wc)].astype(jnp.float32)
-                    + zr[0, slot, :, cols(step, wc)].astype(jnp.float32)
-                ).astype(jnp.bfloat16)
-                inward_copy(step).start()
-
-            @pl.when(step >= LAG)
-            def _():
-                c = step - LAG
+            @pl.when(jnp.logical_and(step == CHUNKS, m + 1 < M))
+            def _():
+                scale(m + 1)
+
+            @pl.when(
+                jnp.logical_and(
+                    m + 1 < M,
+                    jnp.logical_and(step >= CHUNKS, step < CHUNKS + QCHUNKS),
+                )
+            )
+            def _():
+                project(m + 1, step - CHUNKS)
+
+            @pl.when(step >= EARLY + LAG)
+            def _():
+                c = step - EARLY - LAG
                 outward_copy(c).wait_recv()
 
                 @pl.when(middle)
                 def _():
-                    xb[:, cols(c, wc)] = (
-                        xb[:, cols(c, wc)].astype(jnp.float32)
+                    xm[:, cols(c, wc)] = (
+                        xm[:, cols(c, wc)].astype(jnp.float32)
                         + (
                             zs[:, cols(c, wc)].astype(jnp.float32)
                             + zr[1, slot, :, cols(c, wc)].astype(jnp.float32)
@@ -332,7 +384,7 @@
 
                 @pl.when(jnp.logical_not(middle))
                 def _():
-                    xb[:, cols(c, wc)] = zr[1, slot, :, cols(c, wc)]
+                    xm[:, cols(c, wc)] = zr[1, slot, :, cols(c, wc)]
 
                 @pl.when(jnp.logical_not(outer))
                 def _():
@@ -340,7 +392,7 @@
 
                 @pl.when(s == 0)
                 def _():
-                    handed(c).start()
+                    handed(m, c).start()
 
                 @pl.when(jnp.logical_and(s == 1, m < M // 2))
                 def _():
@@ -352,7 +404,7 @@
 
             return 0
 
-        lax.fori_loop(0, CHUNKS + LAG, relay, 0)
+        lax.fori_loop(0, CHUNKS + EARLY + LAG, relay, 0)
 
         def sent(c, _):
             inward_copy(c).wait_send()
@@ -363,7 +415,7 @@
 
             @pl.when(s == 0)
             def _():
-                handed(c).wait_send()
+                handed(m, c).wait_send()
 
             @pl.when(jnp.logical_and(s == 1, m < M // 2))
             def _():
@@ -376,15 +428,7 @@
             return 0
 
         lax.fori_loop(0, CHUNKS, sent, 0)
-
-        def q_sent(j, _):
-            for r in range(D - 1):
-                q_copy(r, j).wait_send()
-            return 0
-
-        lax.fori_loop(0, QCHUNKS, q_sent, 0)
-        for r in range(D - 1):
-            norm_copy(r).wait_send()
+        for r in range(D - 1):
             for h in range(kv_heads):
                 mix_copy(r, h).wait_send()
         return carry
@@ -399,7 +443,7 @@
         def returned(i, _):
             m, c = i // CHUNKS, lax.rem(i, CHUNKS)
             remote(
-                xb.at[:, cols(c, wc)], out.at[rows(m * R, R), cols(c, wc)],
+                xb.at[0, :, cols(c, wc)], out.at[rows(m * R, R), cols(c, wc)],
                 h_s.at[c], h_r.at[m, c], section=1 - s,
             ).wait_recv()
             return 0
@@ -420,13 +464,14 @@
     return pl.pallas_call(
         functools.partial(kernel, D, T),
         out_shape=jax.ShapeDtypeStruct((M // 2 * R, W), bf16),
-        in_specs=[hbm, vmem, vmem, vmem, vmem, hbm, hbm, hbm],
+        in_specs=[hbm, vmem, vmem, vmem, hbm, hbm, hbm],
         out_specs=hbm,
         scratch_shapes=[
             pltpu.VMEM((W, qw), bf16),
             pltpu.VMEM((qcols, W), bf16),
             pltpu.VMEM((M * R, W), bf16),
-            pltpu.VMEM((R, W), bf16),
+            pltpu.VMEM((R, M * R), bf16),
+            pltpu.VMEM((2, R, W), bf16),
             pltpu.VMEM((R, W), bf16),
             pltpu.VMEM((R, qw), bf16),
             pltpu.VMEM((2, D - 1, BLOCK, qw), bf16),
@@ -458,9 +503,8 @@
         ),
     )(
         tokens,
-        order[:, None],
-        segments[:, None],
-        segments.reshape(M * D, BLOCK),
+        order,
+        segments,
         gain,
         w_query[0],
         wkv,

time: 272 us -> 243 us (0.89)
  Pallas kernels: 259 us -> 235 us
  local copies, waits for them, and re-layouts: 12.4 us -> 7.97 us
    pallas_call x1, Pallas kernels: 259 us -> 235 us  [on_device(): pl.pallas_call(functools.partial(kernel, D, T), out_shape=jax.ShapeDtypeS...]
    broadcast_in_dim x2 -> x0, local copies, waits for them, and re-layouts: 3.07 us -> none  [the longest x1 1.54 us: on_device(): segments[:, None]]
where the time goes in v2:
time: 243 us
  Pallas kernels  235 us (97%)
  local copies, waits for them, and re-layouts  7.97 us (3%)
    pallas_call x1, Pallas kernels, on_device(): pl.pallas_call(functools.partial(kernel, D, T), out_shape=jax.ShapeDtypeS...  235 us
    unnamed x2, local copies, waits for them, and re-layouts  7.97 us

profile of v2, /device:TPU:1, one launch (start us, length us, event | category | flops | bytes accessed | tf_op | source)
XLA Modules:
  0.0 242.5 jit_solution(14431685526335048930)
XLA Ops:
  0.0 4.8 %copy.8 = bf16[512,8,2,256]{3,1,2,0:T(8,128)(2,1)} copy(bf16[512,8,2,256]{3,2,1,0:T(2,128)(2,1)} %bitcast.8) | data formatting | bytes 8388608
  4.8 234.6 %shard_map.73 = bf16[256,4096]{1,0:T(8,128)(2,1)} custom-call(bf16[128,16384]{1,0:T(8,128)(2,1)} %tokens.1, s32[512]{0:T(512)} %order.1, s32[512]{0:T(512)} %segments.1, f32[1,4096]{1,0:T(1,128)} %gain.1, bf16[4096,2048]{1,0:T(8,128)(2,1)} %bitcast.5, bf16[4096,512]{1,0:T(8,128)(2,1)} %bitcast.7, bf16[2048,4096]{1,0:T(8,128)(2,1)} %bitcast.6), custom_call_target="tpu_custom_call" | custom-call | tf_op jit(solution)/shard_map/pallas_call | solution.py:464
  239.4 3.1 %copy.10 = bf16[256,4096]{1,0:T(8,128)(2,1)} copy(bf16[256,4096]{1,0:T(8,128)(2,1)} %shard_map.73) | data formatting | bytes 4194304

commit v3 on v2

--- a/solution.py
+++ b/solution.py
@@ -11,8 +11,9 @@
 KEYVALUE_HEADS = 8
 QUERY_HEADS = 64
 HEAD = 128
-BLOCK = 32
-M = 4
+SENTENCE_BLOCK = 32
+BLOCK = 64
+M = 2
 QCHUNKS = 5
 CHUNKS = 8
 EARLY = 3
@@ -46,6 +47,7 @@
     outer = jnp.logical_or(t == 0, t == T - 1)
     middle = jnp.logical_or(t == half - 1, t == half)
     kind = jnp.where(middle, 1, 0)
+    assert BLOCK == 2 * SENTENCE_BLOCK
     kv_heads = KEYVALUE_HEADS // T
     group = QUERY_HEADS // KEYVALUE_HEADS
     qcols = kv_heads * group * HEAD
@@ -228,10 +230,10 @@
             same, jnp.where(mine, 1.0, 0.0).astype(jnp.bfloat16),
             (((1,), (1,)), ((), ())), preferred_element_type=jnp.float32,
         )
-        causal = lax.broadcasted_iota(jnp.int32, (BLOCK, BLOCK), 1) <= (
-            lax.broadcasted_iota(jnp.int32, (BLOCK, BLOCK), 0)
-        )
-        allowed = jnp.where(causal, same, 0.0)
+        there = lax.broadcasted_iota(jnp.int32, (BLOCK, BLOCK), 1)
+        here = lax.broadcasted_iota(jnp.int32, (BLOCK, BLOCK), 0)
+        edge = jnp.where(here >= SENTENCE_BLOCK, SENTENCE_BLOCK, 0)
+        allowed = jnp.where(jnp.logical_and(there <= here, there >= edge), same, 0.0)
         allowed = jnp.concatenate([allowed] * group, axis=0) > 0.5
 
         for r in range(D - 1):
@@ -257,7 +259,7 @@
             return (total / rms).astype(jnp.bfloat16)
 
         def mix_copy(r, h):
-            part = mix.at[slot, own, pl.ds(h * group * HEAD, group * HEAD)]
+            part = mix.at[own, pl.ds(h * group * HEAD, group * HEAD)]
             return remote(
                 part, part, m_s.at[r, h], m_r.at[slot, r, h], dp=peers[r]
             )
@@ -278,7 +280,7 @@
                 jnp.bfloat16
             )
             for g in range(group):
-                mix[slot, own, pl.ds(lower + g * HEAD, HEAD)] = mixed[
+                mix[own, pl.ds(lower + g * HEAD, HEAD)] = mixed[
                     g * BLOCK : (g + 1) * BLOCK
                 ]
             for r in range(D - 1):
@@ -308,19 +310,19 @@
 
         def inward_copy(c):
             return remote(
-                zs.at[:, cols(c, wc)], zr.at[kind, slot, :, cols(c, wc)],
+                zs.at[:, cols(c, wc)], zr.at[kind * (1 + slot), :, cols(c, wc)],
                 z_s.at[c], z_r.at[kind, slot, c], tensor=inward,
             )
 
         def from_outside(c):
             return remote(
-                zs.at[:, cols(c, wc)], zr.at[0, slot, :, cols(c, wc)],
+                zs.at[:, cols(c, wc)], zr.at[0, :, cols(c, wc)],
                 z_s.at[c], z_r.at[0, slot, c], tensor=inward,
             )
 
         def outward_copy(c):
             return remote(
-                xm.at[:, cols(c, wc)], zr.at[1, slot, :, cols(c, wc)],
+                xm.at[:, cols(c, wc)], zr.at[1 + slot, :, cols(c, wc)],
                 t_s.at[c], z_r.at[1, slot, c], tensor=outward,
             )
 
@@ -328,7 +330,7 @@
             @pl.when(step < CHUNKS)
             def _():
                 zs[:, cols(step, wc)] = jnp.dot(
-                    mix[slot], wo_v[:, cols(step, wc)], preferred_element_type=jnp.float32
+                    mix[...], wo_v[:, cols(step, wc)], preferred_element_type=jnp.float32
                 ).astype(jnp.bfloat16)
 
                 @pl.when(outer)
@@ -350,7 +352,7 @@
                 from_outside(c).wait_recv()
                 zs[:, cols(c, wc)] = (
                     zs[:, cols(c, wc)].astype(jnp.float32)
-                    + zr[0, slot, :, cols(c, wc)].astype(jnp.float32)
+                    + zr[0, :, cols(c, wc)].astype(jnp.float32)
                 ).astype(jnp.bfloat16)
                 inward_copy(c).start()
 
@@ -378,13 +380,13 @@
                         xm[:, cols(c, wc)].astype(jnp.float32)
                         + (
                             zs[:, cols(c, wc)].astype(jnp.float32)
-                            + zr[1, slot, :, cols(c, wc)].astype(jnp.float32)
+                            + zr[1 + slot, :, cols(c, wc)].astype(jnp.float32)
                         )
                     ).astype(jnp.bfloat16)
 
                 @pl.when(jnp.logical_not(middle))
                 def _():
-                    xm[:, cols(c, wc)] = zr[1, slot, :, cols(c, wc)]
+                    xm[:, cols(c, wc)] = zr[1 + slot, :, cols(c, wc)]
 
                 @pl.when(jnp.logical_not(outer))
                 def _():
@@ -477,9 +479,9 @@
             pltpu.VMEM((2, D - 1, BLOCK, qw), bf16),
             pltpu.VMEM((R, 128), f32),
             pltpu.VMEM((2, D - 1, BLOCK, 128), f32),
-            pltpu.VMEM((2, R, qcols), bf16),
+            pltpu.VMEM((R, qcols), bf16),
             pltpu.VMEM((R, W), bf16),
-            pltpu.VMEM((2, 2, R, W), bf16),
+            pltpu.VMEM((3, R, W), bf16),
             dma((QCHUNKS,)),
             dma((CHUNKS,)),
             dma,

time: 243 us -> 234 us (0.963)
  Pallas kernels: 235 us -> 225 us
    pallas_call x1, Pallas kernels: 235 us -> 225 us  [on_device(): pl.pallas_call(functools.partial(kernel, D, T), out_shape=jax.ShapeDtypeS...]
where the time goes in v3:
time: 234 us; the launch traced here: 233 us
  Pallas kernels  225 us (96%)
  local copies, waits for them, and re-layouts  7.97 us (3%)
    pallas_call x1, Pallas kernels, on_device(): pl.pallas_call(functools.partial(kernel, D, T), out_shape=jax.ShapeDtypeS...  225 us
    unnamed x2, local copies, waits for them, and re-layouts  7.97 us

profile of v3, /device:TPU:1, one launch (start us, length us, event | category | flops | bytes accessed | tf_op | source)
XLA Modules:
  0.0 233.3 jit_solution(17996322363088657474)
XLA Ops:
  0.0 4.8 %copy.8 = bf16[512,8,2,256]{3,1,2,0:T(8,128)(2,1)} copy(bf16[512,8,2,256]{3,2,1,0:T(2,128)(2,1)} %bitcast.8) | data formatting | bytes 8388608
  4.8 225.3 %shard_map.73 = bf16[256,4096]{1,0:T(8,128)(2,1)} custom-call(bf16[128,16384]{1,0:T(8,128)(2,1)} %tokens.1, s32[512]{0:T(512)} %order.1, s32[512]{0:T(512)} %segments.1, f32[1,4096]{1,0:T(1,128)} %gain.1, bf16[4096,2048]{1,0:T(8,128)(2,1)} %bitcast.5, bf16[4096,512]{1,0:T(8,128)(2,1)} %bitcast.7, bf16[2048,4096]{1,0:T(8,128)(2,1)} %bitcast.6), custom_call_target="tpu_custom_call" | custom-call | tf_op jit(solution)/shard_map/pallas_call | solution.py:466
  230.2 3.1 %copy.10 = bf16[256,4096]{1,0:T(8,128)(2,1)} copy(bf16[256,4096]{1,0:T(8,128)(2,1)} %shard_map.73) | data formatting | bytes 4194304

commit v4 on v3

--- a/solution.py
+++ b/solution.py
@@ -81,11 +81,12 @@
         tokens.at[:, cols(d, W)], ent.at[rows(d * rows_in, rows_in)], own_sem
     )
 
-    def entry(r):
+    def entry(r, c):
         peer = peers[r]
         return remote(
-            tokens.at[:, cols(peer, W)], ent.at[rows(d * rows_in, rows_in)],
-            a_s.at[r], a_r.at[r], dp=peer,
+            tokens.at[:, cols(peer * CHUNKS + c, wc)],
+            ent.at[rows(d * rows_in, rows_in), cols(c, wc)],
+            a_s.at[r, c], a_r.at[r, c], dp=peer,
         )
 
     barrier = pltpu.get_barrier_semaphore()
@@ -105,20 +106,19 @@
 
     @pl.when(s == 0)
     def _():
-        for r in range(D - 1):
-            entry(r).start()
         own_tokens.start()
+
+        def send(c, _):
+            for r in range(D - 1):
+                entry(r, c).start()
+            return 0
+
+        lax.fori_loop(0, CHUNKS, send, 0)
 
     for j in range(QCHUNKS):
         w_copy(j).start()
     for c in range(CHUNKS):
         wo_copy(c).start()
-
-    @pl.when(s == 0)
-    def _():
-        own_tokens.wait()
-        for r in range(D - 1):
-            entry(r).wait_recv()
 
     def handed(n, c):
         return remote(
@@ -152,17 +152,21 @@
             pick[...], ent[:, cols(c, wc)], preferred_element_type=jnp.float32
         ).astype(jnp.bfloat16)
 
-    def scale(n):
-        @pl.when(s == 1)
-        def _():
-            def received(c, _):
+    def scale(n, first=False):
+        def one(c, total):
+            @pl.when(s == 1)
+            def _():
                 handed(n, c).wait_recv()
                 xb[lax.rem(n, 2), :, cols(c, wc)] = ent[rows(n * R, R), cols(c, wc)]
-                return 0
-
-            lax.fori_loop(0, CHUNKS, received, 0)
-
-        def one(c, total):
+
+            if first:
+
+                @pl.when(s == 0)
+                def _():
+                    for r in range(D - 1):
+                        entry(r, c).wait_recv()
+                    take(n, c)
+
             wide = xb[lax.rem(n, 2), :, cols(c, wc)].astype(jnp.float32)
             sc[:, cols(c, wc)] = (wide * gain[:, cols(c, wc)]).astype(jnp.bfloat16)
             square = wide * wide
@@ -184,14 +188,9 @@
     @pl.when(s == 0)
     def _():
         choose(0)
-
-        def first_take(c, _):
-            take(0, c)
-            return 0
-
-        lax.fori_loop(0, CHUNKS, first_take, 0)
-
-    scale(0)
+        own_tokens.wait()
+
+    scale(0, True)
     for j in range(QCHUNKS):
         w_copy(j).wait()
 
@@ -439,8 +438,12 @@
 
     @pl.when(s == 0)
     def _():
-        for r in range(D - 1):
-            entry(r).wait_send()
+        def entered(c, _):
+            for r in range(D - 1):
+                entry(r, c).wait_send()
+            return 0
+
+        lax.fori_loop(0, CHUNKS, entered, 0)
 
         def returned(i, _):
             m, c = i // CHUNKS, lax.rem(i, CHUNKS)
@@ -485,8 +488,8 @@
             dma((QCHUNKS,)),
             dma((CHUNKS,)),
             dma,
-            dma((D - 1,)),
-            dma((D - 1,)),
+            dma((D - 1, CHUNKS)),
+            dma((D - 1, CHUNKS)),
             dma((D - 1, QCHUNKS)),
             dma((2, D - 1, QCHUNKS)),
             dma((D - 1,)),

time: 234 us -> 232 us (level)
  no operation moved by 1% of the time
where the time goes in v4:
time: 232 us
  Pallas kernels  224 us (97%)
  local copies, waits for them, and re-layouts  7.97 us (3%)
    pallas_call x1, Pallas kernels, on_device(): pl.pallas_call(functools.partial(kernel, D, T), out_shape=jax.ShapeDtypeS...  224 us
    unnamed x2, local copies, waits for them, and re-layouts  7.97 us

profile of v4, /device:TPU:1, one launch (start us, length us, event | category | flops | bytes accessed | tf_op | source)
XLA Modules:
  0.0 231.6 jit_solution(14965873242070689768)
XLA Ops:
  0.0 4.8 %copy.8 = bf16[512,8,2,256]{3,1,2,0:T(8,128)(2,1)} copy(bf16[512,8,2,256]{3,2,1,0:T(2,128)(2,1)} %bitcast.8) | data formatting | bytes 8388608
  4.8 223.6 %shard_map.73 = bf16[256,4096]{1,0:T(8,128)(2,1)} custom-call(bf16[128,16384]{1,0:T(8,128)(2,1)} %tokens.1, s32[512]{0:T(512)} %order.1, s32[512]{0:T(512)} %segments.1, f32[1,4096]{1,0:T(1,128)} %gain.1, bf16[4096,2048]{1,0:T(8,128)(2,1)} %bitcast.5, bf16[4096,512]{1,0:T(8,128)(2,1)} %bitcast.7, bf16[2048,4096]{1,0:T(8,128)(2,1)} %bitcast.6), custom_call_target="tpu_custom_call" | custom-call | tf_op jit(solution)/shard_map/pallas_call | solution.py:469
  228.4 3.1 %copy.10 = bf16[256,4096]{1,0:T(8,128)(2,1)} copy(bf16[256,4096]{1,0:T(8,128)(2,1)} %shard_map.73) | data formatting | bytes 4194304
